TPU v7x, 32 devices: a whole 2x2x4 slice. The times are simulated.
32 devices in a mesh: groups: 2 (over y), mp: 4 (over z), dp: 2 (over x), sub: 2 (over core).
Axes of the slice: x: 2, y: 2, z: 4, core: 2. Of those that a mesh axis runs over, the one named last changes fastest.
Arguments:
- gate_act: bfloat16 [5888, 512], P(('mp', 'dp', 'sub'), 'groups'), parts along dimension 1, may hold values from -6 to 6
- up_act: bfloat16 [5888, 512], P(('mp', 'dp', 'sub'), 'groups'), parts along dimension 1, may hold values from -6 to 6
- down_weight: bfloat16 [5888, 16384], P(('mp', 'dp', 'sub')), may hold values from -0.109375 to 0.109375
Outputs:
- mixed: bfloat16 [512, 4, 4096], P('groups', None, ('dp', 'sub')), parts along dimension 0
There are 2 independent parts, one for each index of `groups`. A program takes and returns all parts, laid end to end along the dimension named above; an argument that names none is the same for every part. Nothing has to cross between parts.
All inputs are finite; a program needn't handle non-finite values.
Results may differ from a plain program's by a relative error of at most 0.014.
Values may be sent and summed in bfloat16 or wider, within the bound.
A program may use at most 64 MiB of HBM per device.

v0:
```python
import jax
import jax.numpy as jnp
from jax import lax
from jax.sharding import PartitionSpec as P


def shards(gate_act, up_act, down_weight):
    hidden = (jax.nn.silu(gate_act.astype(jnp.float32)) * up_act.astype(jnp.float32)).astype(
        jnp.bfloat16
    )
    share = lax.psum_scatter(
        lax.dot_general(
            down_weight, hidden, (((0,), (0,)), ((), ())), preferred_element_type=jnp.float32
        ).astype(jnp.bfloat16),
        "mp",
        scatter_dimension=0,
        tiled=True,
    )
    second = lax.psum_scatter(
        share.astype(jnp.float32).astype(jnp.bfloat16),
        ("dp", "sub"),
        scatter_dimension=0,
        tiled=True,
    )
    piece = jnp.transpose(second)[:, None, :]
    return lax.all_gather(piece, "mp", axis=1, tiled=True)


def solution(mesh):
    placed = (
        P(("mp", "dp", "sub"), "groups"),
        P(("mp", "dp", "sub"), "groups"),
        P(("mp", "dp", "sub"), None),
    )
    return jax.shard_map(
        shards,
        mesh=mesh,
        in_specs=placed,
        out_specs=P("groups", None, ("dp", "sub")),
        check_vma=False,
    )
```

profile of v0, /device:TPU:0, one launch (start us, length us, event | category | flops | bytes accessed | tf_op | source)
XLA Modules:
  0.0 259.7 jit_solution(15416458462236350775)
XLA Ops:
  6.5 0.0 reduce-scatter.3.cloned.1.call-start
  6.5 12.5 %fusion = bf16[16384,256]{0,1:T(8,128)(2,1)} fusion(bf16[368,16384]{1,0:T(8,128)(2,1)} %param.5, bf16[368,256]{1,0:T(8,128)(2,1)} %param.4, bf16[368,256]{1,0:T(8,128)(2,1)} %param.3), kind=kOutput, calls=%fused_computation.1 | convolution fusion | flops 3091955712 | bytes 20824064 | tf_op jit(solution)/shard_map/dot_general | solution.py:12
  19.0 0.0 reduce-scatter.3.cloned.1.call-update
  19.0 0.0 reduce-scatter.5.cloned.1.call-start
  19.1 147.3 %reduce-scatter.3.cloned.1.call-done = bf16[4096,256]{0,1:T(8,128)(2,1)} async-done(((bf16[16384,256]{0,1:T(8,128)(2,1)}), bf16[4096,256]{0,1:T(8,128)(2,1)}) %reduce-scatter.3.cloned.1.call-update) | async-done | bytes 2097168 | tf_op jit(solution)/shard_map/reduce_scatter | solution.py:11
  166.3 0.0 reduce-scatter.5.cloned.1.call-update
  166.4 0.0 all-gather.3.cloned.1.call-start
  166.4 34.7 %reduce-scatter.5.cloned.1.call-done = bf16[1024,256]{0,1:T(8,128)(2,1)} async-done(((bf16[4096,256]{0,1:T(8,128)(2,1)}), bf16[1024,256]{0,1:T(8,128)(2,1)}) %reduce-scatter.5.cloned.1.call-update) | async-done | bytes 524304 | tf_op jit(solution)/shard_map/reduce_scatter | solution.py:19
  201.1 0.0 all-gather.3.cloned.1.call-update
  201.1 47.6 %all-gather.3.cloned.1.call-done = bf16[256,4096]{1,0:T(8,128)(2,1)} async-done(((bf16[256,1024]{1,0:T(8,128)(2,1)}), bf16[256,4096]{1,0:T(8,128)(2,1)}) %all-gather.3.cloned.1.call-update) | async-done | bytes 2097168 | tf_op jit(solution)/shard_map/all_gather | solution.py:26
  248.7 4.5 %reshape = bf16[256,4,1024]{2,1,0:T(4,128)(2,1)} reshape(bf16[256,4096]{1,0:T(8,128)(2,1)} %all-gather.3.cloned.1.call-done) | data formatting | bytes 4194304 | tf_op jit(solution)/shard_map/all_gather | solution.py:26
Async XLA Ops:
  6.5 159.8 %reduce-scatter.3.cloned.1.call-start = ((), (), s32[]{:S(2)}) async-start(), calls=%async_computation.2 | async-start | bytes 10485760 | tf_op jit(solution)/shard_map/reduce_scatter | solution.py:11
  19.0 182.0 %reduce-scatter.5.cloned.1.call-start = ((), (), s32[]{:S(2)}) async-start(), calls=%async_computation.3 | async-start | bytes 2621440 | tf_op jit(solution)/shard_map/reduce_scatter | solution.py:19
  166.4 82.3 %all-gather.3.cloned.1.call-start = ((), (), s32[]{:S(2)}) async-start(), calls=%async_computation.4 | async-start | bytes 2621440 | tf_op jit(solution)/shard_map/all_gather | solution.py:26
Sparse Core Ops, SparseCore 0:
  19.1 147.1 reduce-scatter.2
  168.9 32.1 reduce-scatter.4
  202.7 45.9 all-gather.2
where the time goes:
time: 260 us
  waiting for transfers between devices  230 us (88%)
  between operations  13.1 us (5%)
  matrix products  12.5 us (5%)
  local copies, waits for them, and re-layouts  4.48 us (2%)
    reduce_scatter x1, waiting for transfers between devices, shards(): lax.psum_scatter(lax.dot_general(down_weight, hidden, (((0,), (0,)), ((),...  147 us
    all_gather x1, waiting for transfers between devices, shards(): return lax.all_gather(piece, 'mp', axis=1, tiled=True)  47.6 us
    reduce_scatter x1, waiting for transfers between devices, shards(): lax.psum_scatter(share.astype(jnp.float32).astype(jnp.bfloat16), ('dp', '...  34.7 us
    dot_general x1, matrix products, shards(): lax.dot_general(down_weight, hidden, (((0,), (0,)), ((), ())), preferred_...  12.5 us
  transfers between devices with their start and end apart: 3, of which 3 were waited for; matrix products, arithmetic and copies ran while one was open for 0% of the time, Pallas kernels for 0%

commit v1 on v0

v1 whole, which is shorter than its diff:
```python
import functools

import jax
import jax.numpy as jnp
from jax import lax
from jax.experimental import pallas as pl
from jax.experimental.pallas import tpu as pltpu
from jax.sharding import PartitionSpec as P

MESH = pl.DeviceIdType.MESH
F32, BF16 = jnp.float32, jnp.bfloat16

WIDE, TALL = 256, 128
LAG_SUB, LAG_DP, LAG_MP = 2, 2, 2


def kernel(
    sizes, gate, up, weight, out, hidden, held, sub_tx, sub_rx, dp_tx, dp_rx, mp_tx, mp_rx,
    w_sem, sub_send, sub_recv, dp_send, dp_recv, mp_send, mp_recv,
):
    n_mp, n_dp, n_sub = sizes
    depth, rows = gate.shape
    width = out.shape[2]
    wide, tall = mp_tx.shape[2], mp_tx.shape[1]
    per_j, per_c = width // wide, rows // tall
    messages = mp_tx.shape[0]
    z, x, s = lax.axis_index("mp"), lax.axis_index("dp"), lax.axis_index("sub")
    owner = n_mp // 2
    below, above = z < owner, z > owner

    barrier = pltpu.get_barrier_semaphore()
    for i in range(1, n_sub):
        pl.semaphore_signal(barrier, inc=1, device_id={"sub": lax.rem(s + i, n_sub)}, device_id_type=MESH)
    for i in range(1, n_dp):
        pl.semaphore_signal(barrier, inc=1, device_id={"dp": lax.rem(x + i, n_dp)}, device_id_type=MESH)

    @pl.when(z > 0)
    def _():
        pl.semaphore_signal(barrier, inc=1, device_id={"mp": z - 1}, device_id_type=MESH)

    @pl.when(z < n_mp - 1)
    def _():
        pl.semaphore_signal(barrier, inc=1, device_id={"mp": z + 1}, device_id_type=MESH)

    def load(j):
        span = weight.shape[1] // n_mp
        return pltpu.make_async_copy(
            weight.at[:, pl.ds(pl.multiple_of(j * span, 128), span)], held.at[j, pl.ds(0, depth)], w_sem.at[j]
        )

    for j in range(n_mp):
        load(j).start()

    pad = hidden.shape[1] - depth
    if pad:
        for j in range(n_mp):
            held[j, depth:, :] = jnp.zeros((pad, held.shape[2]), BF16)
    for side in range(2):
        mp_rx[side, messages] = jnp.zeros((tall, wide), BF16)
    g, u = gate[...].astype(F32), up[...].astype(F32)
    h = g / (1.0 + jnp.exp(-g)) * u
    if pad:
        h = jnp.concatenate([h, jnp.zeros((pad, rows), F32)], axis=0)
    hidden[...] = jnp.transpose(h).astype(BF16)

    neighbours = jnp.where(z > 0, 1, 0) + jnp.where(z < n_mp - 1, 1, 0)
    pl.semaphore_wait(barrier, n_sub - 1 + n_dp - 1 + neighbours)

    def place(m):
        c, r = m // per_c, m % per_c
        return c // per_j, pl.multiple_of((c % per_j) * wide, 128), pl.multiple_of(r * tall, tall)

    def result(m):
        j, col, row = place(m)
        return out.at[j, pl.ds(row, tall), pl.ds(col, wide)]

    def term(m, d, k):
        j, col, row = place(m)
        first = pl.multiple_of((d * n_sub + k) * width + col, 128)
        return jnp.dot(
            hidden[pl.ds(row, tall), :], held[j, :, pl.ds(first, wide)], preferred_element_type=F32
        )

    def sub_copy(m, i):
        return pltpu.make_async_remote_copy(
            src_ref=sub_tx.at[m, i - 1],
            dst_ref=sub_rx.at[m, n_sub - i - 1],
            send_sem=sub_send.at[i - 1],
            recv_sem=sub_recv.at[m, n_sub - i - 1],
            device_id={"sub": lax.rem(s + i, n_sub)},
            device_id_type=MESH,
        )

    def dp_copy(m, i):
        return pltpu.make_async_remote_copy(
            src_ref=dp_tx.at[m, i - 1],
            dst_ref=dp_rx.at[m, n_dp - i - 1],
            send_sem=dp_send.at[i - 1],
            recv_sem=dp_recv.at[m, n_dp - i - 1],
            device_id={"dp": lax.rem(x + i, n_dp)},
            device_id_type=MESH,
        )

    def mp_copy(src, dst, m, side):
        return pltpu.make_async_remote_copy(
            src_ref=src,
            dst_ref=dst,
            send_sem=mp_send.at[side],
            recv_sem=mp_recv.at[1 - side, m],
            device_id={"mp": z - 1 if side == 0 else z + 1},
            device_id_type=MESH,
        )

    def arrived(ref, sem):
        pltpu.make_async_copy(ref, ref, sem).wait()

    def to_core(m):
        j = m // (per_c * per_j)

        @pl.when(m % (per_c * per_j) == 0)
        def _():
            load(j).wait()

        for i in range(1, n_sub):
            for d in range(n_dp):
                sub_tx[m, i - 1, d] = term(m, d, lax.rem(s + i, n_sub)).astype(BF16)
            sub_copy(m, i).start()

    def to_dp(m):
        for i in range(1, n_sub):
            arrived(sub_rx.at[m, i - 1], sub_recv.at[m, i - 1])
        for i in range(1, n_dp):
            d = lax.rem(x + i, n_dp)
            total = term(m, d, s)
            for k in range(1, n_sub):
                total += sub_rx[m, k - 1, d].astype(F32)
            dp_tx[m, i - 1] = total.astype(BF16)
            dp_copy(m, i).start()

    from_low = (z > 0) & (z <= owner)
    from_high = (z < n_mp - 1) & (z >= owner)

    def to_owner(m):
        total = term(m, x, s)
        for k in range(1, n_sub):
            total += sub_rx[m, k - 1, x].astype(F32)
        for i in range(1, n_dp):
            arrived(dp_rx.at[m, i - 1], dp_recv.at[m, i - 1])
        for i in range(1, n_dp):
            total += dp_rx[m, i - 1].astype(F32)

        @pl.when(from_low)
        def _():
            arrived(mp_rx.at[0, m], mp_recv.at[0, m])

        @pl.when(from_high)
        def _():
            arrived(mp_rx.at[1, m], mp_recv.at[1, m])

        total += mp_rx[0, jnp.where(from_low, m, messages)].astype(F32)
        total += mp_rx[1, jnp.where(from_high, m, messages)].astype(F32)
        summed = total.astype(BF16)

        @pl.when(z == owner)
        def _():
            j, col, row = place(m)
            out[j, pl.ds(row, tall), pl.ds(col, wide)] = summed
            if owner > 0:
                mp_copy(result(m), result(m), m, 0).start()
            if owner < n_mp - 1:
                mp_copy(result(m), result(m), m, 1).start()

        @pl.when(z != owner)
        def _():
            mp_tx[m] = summed

        @pl.when(below)
        def _():
            mp_copy(mp_tx.at[m], mp_rx.at[0, m], m, 1).start()

        @pl.when(above)
        def _():
            mp_copy(mp_tx.at[m], mp_rx.at[1, m], m, 0).start()

    def from_owner(m):
        @pl.when(below)
        def _():
            arrived(result(m), mp_recv.at[1, m])

        @pl.when(above)
        def _():
            arrived(result(m), mp_recv.at[0, m])

        @pl.when(below & (z > 0))
        def _():
            mp_copy(result(m), result(m), m, 0).start()

        @pl.when(above & (z < n_mp - 1))
        def _():
            mp_copy(result(m), result(m), m, 1).start()

    far = max(owner, n_mp - 1 - owner)
    depth_in = jnp.where(z == owner, far, jnp.where(below, z, n_mp - 1 - z))
    depth_out = far + jnp.where(below, owner - z, z - owner)
    lag_in = LAG_SUB + LAG_DP + LAG_MP * depth_in
    lag_out = LAG_SUB + LAG_DP + LAG_MP * depth_out

    def stage(m, work):
        @pl.when((m >= 0) & (m < messages))
        def _():
            work(m)

    def step(t, carry):
        stage(t, to_core)
        stage(t - LAG_SUB, to_dp)
        stage(t - lag_in, to_owner)
        stage(t - lag_out, from_owner)
        return carry

    lax.fori_loop(0, messages + LAG_SUB + LAG_DP + LAG_MP * 2 * far, step, 0)

    for i in range(1, n_sub):
        arrived(sub_tx.at[:, i - 1], sub_send.at[i - 1])
    for i in range(1, n_dp):
        arrived(dp_tx.at[:, i - 1], dp_send.at[i - 1])

    @pl.when(z > 0)
    def _():
        arrived(mp_tx, mp_send.at[0])

    @pl.when(z < n_mp - 1)
    def _():
        arrived(mp_tx, mp_send.at[1])


def solution(mesh):
    n_mp, n_dp, n_sub = (mesh.shape[axis] for axis in ("mp", "dp", "sub"))

    def shards(gate, up, weight):
        depth, rows = gate.shape
        features = weight.shape[1]
        width = features // (n_mp * n_dp * n_sub)
        wide, tall = min(WIDE, width), min(TALL, rows)
        messages = n_mp * (width // wide) * (rows // tall)
        padded = -(-depth // 128) * 128
        parts = pl.pallas_call(
            functools.partial(kernel, (n_mp, n_dp, n_sub)),
            out_shape=jax.ShapeDtypeStruct((n_mp, rows, width), BF16),
            in_specs=[
                pl.BlockSpec(memory_space=pltpu.VMEM),
                pl.BlockSpec(memory_space=pltpu.VMEM),
                pl.BlockSpec(memory_space=pl.ANY),
            ],
            out_specs=pl.BlockSpec(memory_space=pltpu.VMEM),
            scratch_shapes=[
                pltpu.VMEM((rows, padded), BF16),
                pltpu.VMEM((n_mp, padded, features // n_mp), BF16),
                pltpu.VMEM((messages, n_sub - 1, n_dp, tall, wide), BF16),
                pltpu.VMEM((messages, n_sub - 1, n_dp, tall, wide), BF16),
                pltpu.VMEM((messages, n_dp - 1, tall, wide), BF16),
                pltpu.VMEM((messages, n_dp - 1, tall, wide), BF16),
                pltpu.VMEM((messages, tall, wide), BF16),
                pltpu.VMEM((2, messages + 1, tall, wide), BF16),
                pltpu.SemaphoreType.DMA((n_mp,)),
                pltpu.SemaphoreType.DMA((n_sub - 1,)),
                pltpu.SemaphoreType.DMA((messages, n_sub - 1)),
                pltpu.SemaphoreType.DMA((n_dp - 1,)),
                pltpu.SemaphoreType.DMA((messages, n_dp - 1)),
                pltpu.SemaphoreType.DMA((2,)),
                pltpu.SemaphoreType.DMA((2, messages)),
            ],
            compiler_params=pltpu.CompilerParams(
                collective_id=0, has_side_effects=True, vmem_limit_bytes=56 * 1024 * 1024
            ),
            cost_estimate=pl.CostEstimate(
                flops=2 * rows * depth * features,
                bytes_accessed=2 * depth * features,
                transcendentals=rows * depth,
            ),
            name="down_sum",
        )(gate, up, weight)
        return jnp.transpose(parts, (1, 0, 2))

    placed = (
        P(("mp", "dp", "sub"), "groups"),
        P(("mp", "dp", "sub"), "groups"),
        P(("mp", "dp", "sub"), None),
    )
    return jax.shard_map(
        shards,
        mesh=mesh,
        in_specs=placed,
        out_specs=P("groups", None, ("dp", "sub")),
        check_vma=False,
    )
```

time: 260 us -> 81.6 us (0.31)
  waiting for transfers between devices: 230 us -> 0 us
  Pallas kernels: 0 us -> 76.9 us
  between operations: 13.1 us -> 0.01 us
  matrix products: 12.5 us -> 0 us
    reduce_scatter x2 -> x0, waiting for transfers between devices: 182 us -> none  [the longest x1 147 us: shards(): lax.psum_scatter(lax.dot_general(down_weight, hidden, (((0,), (0,)), ((),...]
    pallas_call x0 -> x1, Pallas kernels: none -> 76.9 us  [shards(): pl.pallas_call(functools.partial(kernel, (n_mp, n_dp, n_sub)), out_shape=...]
    all_gather x1 -> x0, waiting for transfers between devices: 47.6 us -> none  [shards(): return lax.all_gather(piece, 'mp', axis=1, tiled=True)]
    dot_general x1 -> x0, matrix products: 12.5 us -> none  [shards(): lax.dot_general(down_weight, hidden, (((0,), (0,)), ((), ())), preferred_...]
    transpose x0 -> x1, local copies, waits for them, and re-layouts: none -> 4.53 us  [shards(): return jnp.transpose(parts, (1, 0, 2))]
    all_gather x1 -> x0, local copies, waits for them, and re-layouts: 4.48 us -> none  [shards(): return lax.all_gather(piece, 'mp', axis=1, tiled=True)]
  transfers between devices with their start and end apart: 3 -> 0, of which waited for: 3 -> 0; matrix products, arithmetic and copies ran while one was open for 0% -> 0% of each run, Pallas kernels for 0% -> 0%
where the time goes in v1:
time: 81.6 us; the launch traced here: 81.4 us
  Pallas kernels  76.9 us (94%)
  local copies, waits for them, and re-layouts  4.53 us (6%)
    pallas_call x1, Pallas kernels, shards(): pl.pallas_call(functools.partial(kernel, (n_mp, n_dp, n_sub)), out_shape=...  76.9 us
    transpose x1, local copies, waits for them, and re-layouts, shards(): return jnp.transpose(parts, (1, 0, 2))  4.53 us

profile of v1, /device:TPU:0, one launch (start us, length us, event | category | flops | bytes accessed | tf_op | source)
XLA Modules:
  0.0 81.4 jit_solution(7138633351089186986)
XLA Ops:
  0.0 76.9 %down_sum.1 = bf16[4,256,1024]{2,1,0:T(8,128)(2,1)} custom-call(bf16[368,256]{1,0:T(8,128)(2,1)} %gate.1, bf16[368,256]{1,0:T(8,128)(2,1)} %up.1, bf16[368,16384]{1,0:T(8,128)(2,1)} %weight.1), custom_call_target="tpu_custom_call" | custom-call | flops 3087007744 | bytes 12058624 | tf_op jit(solution)/shard_map/down_sum/pallas_call | solution.py:246
  76.9 4.5 %copy.4 = bf16[256,4,1024]{2,1,0:T(4,128)(2,1)} copy(bf16[256,4,1024]{2,0,1:T(8,128)(2,1)} %bitcast.1) | data formatting | bytes 4194304 | tf_op jit(solution)/shard_map/transpose | solution.py:282

commit v2 on v1

v2 whole, which is shorter than its diff:
```python
import functools

import jax
import jax.numpy as jnp
from jax import lax
from jax.experimental import pallas as pl
from jax.experimental.pallas import tpu as pltpu
from jax.sharding import PartitionSpec as P

MESH = pl.DeviceIdType.MESH
F32, BF16 = jnp.float32, jnp.bfloat16

WIDE, TALL = 256, 64
LAG_DP, LAG_MP = 5, 5


def kernel(
    sizes, gate, up, weight, out, hidden, held, sub_tx, sub_rx, dp_tx, dp_rx, own, mp_tx, mp_rx, done,
    w_sem, sub_send, sub_recv, dp_send, dp_recv, mp_send, mp_recv,
):
    n_mp, n_dp, n_sub = sizes
    depth, rows = gate.shape
    width = out.shape[2]
    messages, tall, wide = mp_tx.shape
    chunks = held.shape[0]
    per_c = rows // tall
    z, x, s = lax.axis_index("mp"), lax.axis_index("dp"), lax.axis_index("sub")
    owner = n_mp // 2
    below, above = z < owner, z > owner

    barrier = pltpu.get_barrier_semaphore()
    for i in range(1, n_sub):
        pl.semaphore_signal(barrier, inc=1, device_id={"sub": lax.rem(s + i, n_sub)}, device_id_type=MESH)
    for i in range(1, n_dp):
        pl.semaphore_signal(barrier, inc=1, device_id={"dp": lax.rem(x + i, n_dp)}, device_id_type=MESH)

    @pl.when(z > 0)
    def _():
        pl.semaphore_signal(barrier, inc=1, device_id={"mp": z - 1}, device_id_type=MESH)

    @pl.when(z < n_mp - 1)
    def _():
        pl.semaphore_signal(barrier, inc=1, device_id={"mp": z + 1}, device_id_type=MESH)

    def load(c):
        for q in range(n_dp * n_sub):
            first = ((c % n_mp) * n_dp * n_sub + q) * width + (c // n_mp) * wide
            pltpu.make_async_copy(
                weight.at[:, pl.ds(pl.multiple_of(first, 128), wide)],
                held.at[c, pl.ds(0, depth), pl.ds(q * wide, wide)],
                w_sem.at[c],
            ).start()

    lax.fori_loop(0, chunks, lambda c, carry: (load(c), carry)[1], 0)

    pad = hidden.shape[1] - depth
    if pad:
        for c in range(chunks):
            held[c, depth:, :] = jnp.zeros((pad, held.shape[2]), BF16)
    for side in range(2):
        mp_rx[side, messages] = jnp.zeros((tall, wide), BF16)
    g, u = gate[...].astype(F32), up[...].astype(F32)
    h = g / (1.0 + jnp.exp(-g)) * u
    if pad:
        h = jnp.concatenate([h, jnp.zeros((pad, rows), F32)], axis=0)
    hidden[...] = jnp.transpose(h).astype(BF16)

    neighbours = jnp.where(z > 0, 1, 0) + jnp.where(z < n_mp - 1, 1, 0)
    pl.semaphore_wait(barrier, n_sub - 1 + n_dp - 1 + neighbours)

    def term(c, d, k):
        first = pl.multiple_of((d * n_sub + k) * wide, 128)
        return jnp.dot(hidden[...], held[c, :, pl.ds(first, wide)], preferred_element_type=F32)

    def sub_copy(c, i):
        return pltpu.make_async_remote_copy(
            src_ref=sub_tx.at[c, i - 1],
            dst_ref=sub_rx.at[c, n_sub - i - 1],
            send_sem=sub_send.at[i - 1],
            recv_sem=sub_recv.at[c, n_sub - i - 1],
            device_id={"sub": lax.rem(s + i, n_sub)},
            device_id_type=MESH,
        )

    def dp_copy(m, i):
        return pltpu.make_async_remote_copy(
            src_ref=dp_tx.at[i - 1, m],
            dst_ref=dp_rx.at[n_dp - i - 1, m],
            send_sem=dp_send.at[i - 1],
            recv_sem=dp_recv.at[n_dp - i - 1, m],
            device_id={"dp": lax.rem(x + i, n_dp)},
            device_id_type=MESH,
        )

    def mp_copy(src, dst, m, side):
        return pltpu.make_async_remote_copy(
            src_ref=src,
            dst_ref=dst,
            send_sem=mp_send.at[side],
            recv_sem=mp_recv.at[1 - side, m],
            device_id={"mp": z - 1 if side == 0 else z + 1},
            device_id_type=MESH,
        )

    def arrived(ref, sem):
        pltpu.make_async_copy(ref, ref, sem).wait()

    def to_core(c):
        arrived(held.at[c, pl.ds(0, depth)], w_sem.at[c])
        for i in range(1, n_sub):
            for d in range(n_dp):
                sub_tx[c, i - 1, d] = term(c, d, lax.rem(s + i, n_sub)).astype(BF16)
            sub_copy(c, i).start()

    def chip_term(c, d):
        total = term(c, d, s)
        for k in range(1, n_sub):
            total += sub_rx[c, k - 1, d].astype(F32)
        return total

    def to_dp(c):
        for i in range(1, n_sub):
            arrived(sub_rx.at[c, i - 1], sub_recv.at[c, i - 1])
        for i in range(1, n_dp):
            total = chip_term(c, lax.rem(x + i, n_dp)).astype(BF16)
            for r in range(per_c):
                dp_tx[i - 1, c * per_c + r] = total[r * tall : (r + 1) * tall]
                dp_copy(c * per_c + r, i).start()

    def keep(c):
        total = chip_term(c, x)
        for r in range(per_c):
            own[c * per_c + r] = total[r * tall : (r + 1) * tall]

    from_low = (z > 0) & (z <= owner)
    from_high = (z < n_mp - 1) & (z >= owner)

    def to_owner(m):
        for i in range(1, n_dp):
            arrived(dp_rx.at[i - 1, m], dp_recv.at[i - 1, m])

        @pl.when(from_low)
        def _():
            arrived(mp_rx.at[0, m], mp_recv.at[0, m])

        @pl.when(from_high)
        def _():
            arrived(mp_rx.at[1, m], mp_recv.at[1, m])

        total = own[m]
        for i in range(1, n_dp):
            total += dp_rx[i - 1, m].astype(F32)
        total += mp_rx[0, jnp.where(from_low, m, messages)].astype(F32)
        total += mp_rx[1, jnp.where(from_high, m, messages)].astype(F32)
        summed = total.astype(BF16)

        @pl.when(z == owner)
        def _():
            done[m] = summed
            if owner > 0:
                mp_copy(done.at[m], done.at[m], m, 0).start()
            if owner < n_mp - 1:
                mp_copy(done.at[m], done.at[m], m, 1).start()
            write(m)

        @pl.when(z != owner)
        def _():
            mp_tx[m] = summed

        @pl.when(below)
        def _():
            mp_copy(mp_tx.at[m], mp_rx.at[0, m], m, 1).start()

        @pl.when(above)
        def _():
            mp_copy(mp_tx.at[m], mp_rx.at[1, m], m, 0).start()

    def write(m):
        c, r = m // per_c, m % per_c

        @pl.when(c % n_mp == n_mp - 1)
        def _():
            blocks = [done[m - (n_mp - 1 - j) * per_c].astype(F32) for j in range(n_mp)]
            col = pl.multiple_of((c // n_mp) * wide, 128)
            out[pl.ds(r * tall, tall), :, pl.ds(col, wide)] = jnp.stack(blocks, axis=1).astype(BF16)

    def from_owner(m):
        @pl.when(below)
        def _():
            arrived(done.at[m], mp_recv.at[1, m])

        @pl.when(above)
        def _():
            arrived(done.at[m], mp_recv.at[0, m])

        @pl.when(below & (z > 0))
        def _():
            mp_copy(done.at[m], done.at[m], m, 0).start()

        @pl.when(above & (z < n_mp - 1))
        def _():
            mp_copy(done.at[m], done.at[m], m, 1).start()

        @pl.when(z != owner)
        def _():
            write(m)

    far = max(owner, n_mp - 1 - owner)
    depth_in = jnp.where(z == owner, far, jnp.where(below, z, n_mp - 1 - z))
    depth_out = far + jnp.where(below, owner - z, z - owner)
    lag_in = per_c + LAG_DP + LAG_MP * depth_in
    lag_out = per_c + LAG_DP + LAG_MP * depth_out

    def stage(m, count, work):
        @pl.when((m >= 0) & (m < count))
        def _():
            work(m)

    def step(k, carry):
        for r in range(per_c):
            if r == 0:
                stage(k, chunks, to_core)
            if r == min(1, per_c - 1):
                stage(k - 1, chunks, to_dp)
            if r == min(2, per_c - 1):
                stage(k - 1, chunks, keep)
            stage(k * per_c + r - lag_in, messages, to_owner)
            stage(k * per_c + r - lag_out, messages, from_owner)
        return carry

    last = messages + per_c + LAG_DP + LAG_MP * 2 * far
    lax.fori_loop(0, -(-last // per_c), step, 0)

    for i in range(1, n_sub):
        arrived(sub_tx.at[:, i - 1], sub_send.at[i - 1])
    for i in range(1, n_dp):
        arrived(dp_tx.at[i - 1], dp_send.at[i - 1])

    @pl.when(z > 0)
    def _():
        arrived(mp_tx, mp_send.at[0])

    @pl.when(z < n_mp - 1)
    def _():
        arrived(mp_tx, mp_send.at[1])


def solution(mesh):
    n_mp, n_dp, n_sub = (mesh.shape[axis] for axis in ("mp", "dp", "sub"))

    def shards(gate, up, weight):
        depth, rows = gate.shape
        features = weight.shape[1]
        width = features // (n_mp * n_dp * n_sub)
        wide, tall = min(WIDE, width), min(TALL, rows)
        chunks = n_mp * (width // wide)
        messages = chunks * (rows // tall)
        padded = -(-depth // 128) * 128
        return pl.pallas_call(
            functools.partial(kernel, (n_mp, n_dp, n_sub)),
            out_shape=jax.ShapeDtypeStruct((rows, n_mp, width), BF16),
            in_specs=[
                pl.BlockSpec(memory_space=pltpu.VMEM),
                pl.BlockSpec(memory_space=pltpu.VMEM),
                pl.BlockSpec(memory_space=pl.ANY),
            ],
            out_specs=pl.BlockSpec(memory_space=pltpu.VMEM),
            scratch_shapes=[
                pltpu.VMEM((rows, padded), BF16),
                pltpu.VMEM((chunks, padded, n_dp * n_sub * wide), BF16),
                pltpu.VMEM((chunks, n_sub - 1, n_dp, rows, wide), BF16),
                pltpu.VMEM((chunks, n_sub - 1, n_dp, rows, wide), BF16),
                pltpu.VMEM((n_dp - 1, messages, tall, wide), BF16),
                pltpu.VMEM((n_dp - 1, messages, tall, wide), BF16),
                pltpu.VMEM((messages, tall, wide), F32),
                pltpu.VMEM((messages, tall, wide), BF16),
                pltpu.VMEM((2, messages + 1, tall, wide), BF16),
                pltpu.VMEM((messages, tall, wide), BF16),
                pltpu.SemaphoreType.DMA((chunks,)),
                pltpu.SemaphoreType.DMA((n_sub - 1,)),
                pltpu.SemaphoreType.DMA((chunks, n_sub - 1)),
                pltpu.SemaphoreType.DMA((n_dp - 1,)),
                pltpu.SemaphoreType.DMA((n_dp - 1, messages)),
                pltpu.SemaphoreType.DMA((2,)),
                pltpu.SemaphoreType.DMA((2, messages)),
            ],
            compiler_params=pltpu.CompilerParams(
                collective_id=0, has_side_effects=True, vmem_limit_bytes=56 * 1024 * 1024
            ),
            cost_estimate=pl.CostEstimate(
                flops=2 * rows * depth * features,
                bytes_accessed=2 * depth * features,
                transcendentals=rows * depth,
            ),
            name="down_sum",
        )(gate, up, weight)

    placed = (
        P(("mp", "dp", "sub"), "groups"),
        P(("mp", "dp", "sub"), "groups"),
        P(("mp", "dp", "sub"), None),
    )
    return jax.shard_map(
        shards,
        mesh=mesh,
        in_specs=placed,
        out_specs=P("groups", None, ("dp", "sub")),
        check_vma=False,
    )
```

time: 81.6 us -> 73.5 us (0.901)
  Pallas kernels: 76.9 us -> 69.7 us
  local copies, waits for them, and re-layouts: 4.53 us -> 3.63 us
    pallas_call x1, Pallas kernels: 76.9 us -> 69.7 us  [shards(): pl.pallas_call(functools.partial(kernel, (n_mp, n_dp, n_sub)), out_shape=...]
    transpose x1 -> x0, local copies, waits for them, and re-layouts: 4.53 us -> none  [shards(): return jnp.transpose(parts, (1, 0, 2))]
    unnamed x0 -> x1, local copies, waits for them, and re-layouts: none -> 3.63 us
where the time goes in v2:
time: 73.5 us; the launch traced here: 73.3 us
  Pallas kernels  69.7 us (95%)
  local copies, waits for them, and re-layouts  3.63 us (5%)
    pallas_call x1, Pallas kernels, shards(): pl.pallas_call(functools.partial(kernel, (n_mp, n_dp, n_sub)), out_shape=...  69.7 us
    unnamed x1, local copies, waits for them, and re-layouts  3.63 us

profile of v2, /device:TPU:0, one launch (start us, length us, event | category | flops | bytes accessed | tf_op | source)
XLA Modules:
  0.0 73.3 jit_solution(3305254406232125248)
XLA Ops:
  0.0 69.7 %down_sum.1 = bf16[256,4,1024]{2,1,0:T(4,128)(2,1)} custom-call(bf16[368,256]{1,0:T(8,128)(2,1)} %gate.1, bf16[368,256]{1,0:T(8,128)(2,1)} %up.1, bf16[368,16384]{1,0:T(8,128)(2,1)} %weight.1), custom_call_target="tpu_custom_call" | custom-call | flops 3087007744 | bytes 12058624 | tf_op jit(solution)/shard_map/down_sum/pallas_call | solution.py:259
  69.7 3.6 %copy.5 = bf16[256,4,1024]{2,1,0:T(4,128)(2,1)} copy(bf16[256,4,1024]{2,1,0:T(4,128)(2,1)} %down_sum.1) | data formatting | bytes 4194304
